TPU v7x, 32 devices: a whole 2x2x4 slice. The times are simulated.
32 devices in a mesh: mapx: 8 (over z, x), mapy: 2 (over y), layer: 2 (over core).
Axes of the slice: x: 2, y: 2, z: 4, core: 2. Of those that a mesh axis runs over, the one named last changes fastest.
Arguments:
- old_state: float32 [8, 2, 2, 6, 8192], P('mapx', 'mapy', 'layer'), as said below
- send_blocks: int32 [8, 2, 2, 10, 16], P('mapx', 'mapy', 'layer'), may hold values from 0 to 63
- node_slots: int32 [8, 2, 2, 4, 512], P('mapx', 'mapy', 'layer'), may hold values from 0 to 20479, as said below
- node_weights: float32 [8, 2, 2, 4, 512], P('mapx', 'mapy', 'layer'), as said below
- front_mask: int32 [8, 2, 2, 512], P('mapx', 'mapy', 'layer'), may hold values 0 or 1
- halo_lists: int32 [8, 2, 2, 6, 256], P('mapx', 'mapy', 'layer'), may hold values from 0 to 511
- elem_nodes: int32 [8, 2, 2, 4, 2560], P('mapx', 'mapy', 'layer'), may hold values from 0 to 2047
- shape_grads: float32 [8, 2, 2, 12, 2560], P('mapx', 'mapy', 'layer'), as said below
- elem_volume: float32 [8, 2, 2, 2560], P('mapx', 'mapy', 'layer'), may hold values from 0.5 to 2
Outputs:
- new_state: float32 [8, 2, 2, 6, 512], P('mapx', 'mapy', 'layer')
- residual: float32 [8, 2, 2, 4, 512], P('mapx', 'mapy', 'layer')
Inputs may be any that keep to these rules, and one draw needn't show every extreme that they name: `send_blocks`: each entry names one of the sender's old blocks; a block may go to several peers or twice to one. `node_slots`: indexes the received nodes, ordered by source (mapx offset plus 2, times 2, plus layer index), then slot, then node in the block; only sources inside the device grid are named. `node_weights`: Positive; the four weights of a node sum to one. `halo_lists`: owned nodes kept as ghosts by the neighbour in direction k. `elem_nodes`: local numbering: the owned nodes first, then 256 ghosts for each of the six directions in order. `shape_grads`: the four gradients of an element sum to zero. `old_state`: rows 0 to 3 velocity and pressure, row 4 temperature in [-1, 0], row 5 damage in [0, 0.9].
All inputs are finite; a program needn't handle non-finite values. No bound on the sum of `front_mask` on one device may be relied on, other than what follows from the above.
Results may differ from a plain program's by a relative error of at most 0.00002.
Values sent between devices are 32-bit elements; how exact they have to be, the bound alone decides.
No kernel may reach another device: no remote copies, remote signals or barrier semaphores. Data moves between devices by JAX's collectives and lax.ppermute only.
A program may use at most 64 MiB of HBM per device.

v0:
```python
import functools

import jax
import jax.numpy as jnp
from jax import lax
from jax.experimental import pallas as pl
from jax.experimental.pallas import tpu as pltpu
from jax.sharding import PartitionSpec as P

BLOCK = 128
REACH = 2
FIELDS = 6
SPLITS = 3

ocean_temp = 0.0
strain_reg = 0.01
gravity = 0.5

AXES = ("mapx", "mapy", "layer")
VMEM = pl.BlockSpec(memory_space=pltpu.VMEM)
SMEM = pl.BlockSpec(memory_space=pltpu.SMEM)


def params():
    return pltpu.CompilerParams(vmem_limit_bytes=32 * 1024 * 1024)


def near_groups(sizes):
    nx, ny, nl = sizes
    number = lambda x, y, l: (x * ny + y) * nl + l
    return [
        [number(first + i, y, l) for i in range(4) for l in range(nl)] for first in range(0, nx, 4) for y in range(ny)
    ]


def both_ways(pairs):
    return [way for one, other in pairs for way in ((one, other), (other, one))]


def far_pairs(count):
    two, one = [], []
    for first in range(2, count - 3, 4):
        two += [(first, first + 2), (first + 1, first + 3)]
        one += [(first + 1, first + 2)]
    return both_ways(two), both_ways(one)


def pair_groups(sizes):
    nx, ny, nl = sizes
    number = lambda x, y, l: (x * ny + y) * nl + l
    return [
        [number(x + i, y + j, l) for i in range(2) for j in range(2) for l in range(2)]
        for x in range(0, nx, 2)
        for y in range(0, ny, 2)
    ]


def group_swap(chunks, groups):
    return lax.all_to_all(chunks, AXES, split_axis=0, concat_axis=0, axis_index_groups=groups)


def far_swap(value, axis, count):
    pairs = []
    for first in range(1, count - 1, 2):
        pairs += [(first, first + 1), (first + 1, first)]
    return lax.ppermute(value, axis, pairs)


def put_blocks(blocks_ref, old_ref, out_ref, chunk, peer):
    slots = blocks_ref.shape[1]
    count = old_ref.shape[0] // FIELDS
    for c in range(slots):
        rows = pl.ds(blocks_ref[peer, c], FIELDS, stride=count)
        out_ref[chunk, FIELDS * c : FIELDS * (c + 1), :] = old_ref[rows, :]


def far_place():
    at = lax.rem(lax.axis_index("mapx") + 2, 4)
    return at, jnp.where(at < 2, 1, -1)


def pack_far_kernel(blocks_ref, old_ref, swap_ref, own_ref):
    layer = lax.axis_index("layer")
    _, way = far_place()
    for i in range(2):
        peer = ((REACH - i) * way + REACH) * 2
        put_blocks(blocks_ref, old_ref, swap_ref, i, peer + 1 - layer)
    for i in range(2):
        peer = ((REACH - i) * way + REACH) * 2
        put_blocks(blocks_ref, old_ref, own_ref, i, peer + layer)


def pack_near_kernel(blocks_ref, old_ref, near_ref):
    here = lax.rem(lax.axis_index("mapx"), 4)

    def near(chunk, carry):
        offset = chunk // 2 - here

        @pl.when(jnp.abs(offset) <= REACH)
        def _():
            put_blocks(blocks_ref, old_ref, near_ref, chunk, (offset + REACH) * 2 + lax.rem(chunk, 2))

        return carry

    lax.fori_loop(0, 8, near, 0)


def pick(row, lanes):
    return jnp.take_along_axis(jnp.broadcast_to(row, lanes.shape), lanes, axis=1)


def add_blocks(chunk_ref, chunk, first_block, slots, blocks, lanes, found):
    parts = len(blocks)
    local = [blocks[v] - first_block for v in range(parts)]
    found = list(found)
    for c in range(slots):
        hit = [local[v] == c for v in range(parts)]
        for f in range(FIELDS):
            row = chunk_ref[chunk, FIELDS * c + f : FIELDS * c + f + 1, :]
            for v in range(parts):
                found[f * parts + v] = jnp.where(hit[v], pick(row, lanes[v]), found[f * parts + v])
    return tuple(found)


def near_kernel(near_ref, slots_ref, found_ref):
    slots = near_ref.shape[1] // FIELDS
    parts = slots_ref.shape[0] // 8
    ids = [slots_ref[8 * v : 8 * v + 8, :] for v in range(parts)]
    blocks = [i >> 7 for i in ids]
    lanes = [i & (BLOCK - 1) for i in ids]
    here = lax.rem(lax.axis_index("mapx"), 4)

    def step(chunk, found):
        source = (chunk // 2 - here + REACH) * 2 + lax.rem(chunk, 2)
        return add_blocks(near_ref, chunk, source * slots, slots, blocks, lanes, found)

    start = tuple(jnp.zeros((8, BLOCK), jnp.float32) for _ in range(FIELDS * parts))
    found = lax.fori_loop(0, 8, step, start)
    for f in range(FIELDS):
        for v in range(parts):
            found_ref[f, 8 * v : 8 * v + 8, :] = found[f * parts + v]


def state_kernel(
    two_ref, one_ref, slots_ref, found_ref, weights_ref, mask_ref, halos_ref, state_ref, table_ref, group_ref, far_x_ref, far_y_ref, cut_ref
):
    slots = two_ref.shape[1] // FIELDS
    parts = slots_ref.shape[0] // 8
    ids = [slots_ref[8 * v : 8 * v + 8, :] for v in range(parts)]
    blocks = [i >> 7 for i in ids]
    lanes = [i & (BLOCK - 1) for i in ids]
    at, way = far_place()
    found = tuple(found_ref[f, 8 * v : 8 * v + 8, :] for f in range(FIELDS) for v in range(parts))
    first_two = (2 * way + REACH) * 2 * slots
    first_one = jnp.where((at == 1) | (at == 2), (way + REACH) * 2 * slots, -(1 << 20))
    for ref, first in ((two_ref, first_two), (one_ref, first_one)):

        def step(chunk, found, ref=ref, first=first):
            return add_blocks(ref, chunk, first + chunk * slots, slots, blocks, lanes, found)

        found = lax.fori_loop(0, 2, step, found)
    front = mask_ref[...] == 1
    rows = mask_ref.shape[0]
    for f in range(FIELDS):
        total = jnp.zeros((rows, BLOCK), jnp.float32)
        for v in range(parts):
            term = found[f * parts + v] * weights_ref[8 * v : 8 * v + 8, :]
            for k in range(8 // rows):
                total = total + term[k * rows : (k + 1) * rows, :]
        if f == 4:
            total = jnp.where(front, ocean_temp, total)
        for r in range(rows):
            state_ref[f : f + 1, r * BLOCK : (r + 1) * BLOCK] = total[r : r + 1, :]
        for s in range(rows // 2):
            table_ref[s, 2 * f : 2 * f + 2, :] = total[2 * s : 2 * s + 2, :]
    halo_parts = halos_ref.shape[0] // 8
    halo = [halos_ref[8 * v : 8 * v + 8, :] for v in range(halo_parts)]
    halo_blocks = [i >> 7 for i in halo]
    halo_lanes = [i & (BLOCK - 1) for i in halo]
    for f in range(FIELDS):
        cut = [jnp.zeros((8, BLOCK), jnp.float32) for _ in range(halo_parts)]
        for b in range(rows):
            row = table_ref[b // 2, 2 * f + b % 2 : 2 * f + b % 2 + 1, :]
            for v in range(halo_parts):
                cut[v] = jnp.where(halo_blocks[v] == b, pick(row, halo_lanes[v]), cut[v])
        for k in range(6):
            v, r = (2 * k) // 8, (2 * k) % 8
            cut_ref[k, 2 * f : 2 * f + 2, :] = cut[v][r : r + 2, :]
    send_pairs(cut_ref, group_ref, far_x_ref, far_y_ref, [(0, 1), (2, 3), (4, 5)])


def pair_places():
    return [lax.rem(lax.axis_index(axis), 2) for axis in AXES]


def partner(px, py, pz, axis):
    flip = [px, py, pz]
    flip[axis] = 1 - flip[axis]
    return flip[0] * 4 + flip[1] * 2 + flip[2]


def send_pairs(cut_ref, group_ref, far_x_ref, far_y_ref, order):
    places = pair_places()
    for axis in range(3):
        even, odd = order[axis]
        inside = jnp.where(places[axis] == 0, even, odd)
        outside = jnp.where(places[axis] == 0, odd, even)
        group_ref[partner(*places, axis)] = cut_ref[inside]
        if axis == 0:
            far_x_ref[...] = cut_ref[outside]
        if axis == 1:
            far_y_ref[...] = cut_ref[outside]


def arrivals(group_ref, far_refs, counts):
    places = pair_places()
    result = []
    for axis in range(3):
        inside = group_ref[partner(*places, axis)]
        at = lax.axis_index(AXES[axis])
        edge = jnp.where(places[axis] == 0, at == 0, at == counts[axis] - 1)
        if far_refs[axis] is None:
            outside = jnp.zeros_like(inside)
        else:
            outside = jnp.where(edge, 0.0, far_refs[axis][...])
        result.append((places[axis], inside, outside))
    return result


def one_hot_sum(values, ids, block_count):
    rows = lax.broadcasted_iota(jnp.int32, (block_count, BLOCK), 0)
    hit = rows == jnp.broadcast_to(ids >> 7, rows.shape)
    left = [jnp.where(hit, jnp.broadcast_to(v, rows.shape), 0.0) for v in values]
    left = jnp.concatenate(left, axis=0).astype(jnp.bfloat16)
    lanes = lax.broadcasted_iota(jnp.int32, (BLOCK, BLOCK), 0)
    right = jnp.where(lanes == jnp.broadcast_to(ids & (BLOCK - 1), lanes.shape), 1.0, 0.0).astype(jnp.bfloat16)
    return left, right


def cut_parts(value):
    parts = []
    for _ in range(SPLITS - 1):
        part = value.astype(jnp.bfloat16).astype(jnp.float32)
        parts.append(part)
        value = value - part
    return parts + [value]


def nt_dot(left, right):
    return lax.dot_general(left, right, (((1,), (1,)), ((), ())), preferred_element_type=jnp.float32)


def element_kernel(
    counts,
    elem_rows,
    table_in_ref,
    group_ref,
    far_x_ref,
    far_y_ref,
    nodes_ref,
    grads_ref,
    volume_ref,
    own_ref,
    back_ref,
    back_x_ref,
    back_y_ref,
    table_ref,
    parts_ref,
    cut_ref,
):
    owned_slots = table_in_ref.shape[0]
    table_ref[0:owned_slots] = table_in_ref[...]
    far_refs = [far_x_ref, far_y_ref if counts[1] > 2 else None, None]
    for axis, (place_at, inside, outside) in enumerate(arrivals(group_ref, far_refs, counts)):
        table_ref[owned_slots + 2 * axis + 1 - place_at] = inside
        table_ref[owned_slots + 2 * axis + place_at] = outside
    block_count = 2 * table_ref.shape[0]
    padded = nodes_ref.shape[1]
    for t in range(padded // 8):
        at = slice(8 * t, 8 * t + 8)
        values = []
        for a in range(4):
            ids = nodes_ref[a, at, :]
            blocks, lanes = ids >> 7, ids & (BLOCK - 1)
            found = [jnp.zeros((8, BLOCK), jnp.float32) for _ in range(FIELDS)]
            for b in range(block_count):
                hit = blocks == b
                for f in range(FIELDS):
                    row = table_ref[b // 2, 2 * f + b % 2 : 2 * f + b % 2 + 1, :]
                    found[f] = jnp.where(hit, pick(row, lanes), found[f])
            values.append(found)
        grads = [[grads_ref[3 * a + j, at, :] for j in range(3)] for a in range(4)]
        volume = volume_ref[at, :]
        velgrad = [[sum(values[a][i] * grads[a][j] for a in range(4)) for j in range(3)] for i in range(3)]
        strain = [[0.5 * (velgrad[i][j] + velgrad[j][i]) if i <= j else None for j in range(3)] for i in range(3)]
        diagonal = sum(strain[i][i] * strain[i][i] for i in range(3))
        corner = sum(strain[i][j] * strain[i][j] for i, j in ((0, 1), (0, 2), (1, 2)))
        second = 0.5 * diagonal + corner
        pressure, temper, damage = [0.25 * (values[0][f] + values[1][f] + values[2][f] + values[3][f]) for f in (3, 4, 5)]
        root = jnp.exp(jnp.log(second + strain_reg) * (-1.0 / 3.0))
        twice = (1.0 - damage) * jnp.exp(-temper) * root
        stress = [[None] * 3 for _ in range(3)]
        for i in range(3):
            for j in range(i, 3):
                stress[i][j] = twice * strain[i][j] - (pressure if i == j else 0.0)
                stress[j][i] = stress[i][j]
        lift = (0.25 * gravity) * volume
        flow = 0.25 * volume * (velgrad[0][0] + velgrad[1][1] + velgrad[2][2])
        for s, part in enumerate(cut_parts(flow)):
            for a in range(4):
                parts_ref[3 * SPLITS + s, a * padded + 8 * t : a * padded + 8 * t + 8, :] = part
        for a in range(4):
            for i in range(3):
                force = volume * sum(stress[i][j] * grads[a][j] for j in range(3))
                if i == 2:
                    force = force + lift
                for s, part in enumerate(cut_parts(force)):
                    parts_ref[i * SPLITS + s, a * padded + 8 * t : a * padded + 8 * t + 8, :] = part

    group = 10

    def gather_terms(step, total):
        a = step // (elem_rows // group)
        first = lax.rem(step, elem_rows // group) * group
        lefts, rights = [], []
        for r in range(group):
            ids = nodes_ref[a, pl.ds(first + r, 1), :]
            terms = [
                parts_ref[c * SPLITS + s, pl.ds(a * padded + first + r, 1), :] for s in range(SPLITS) for c in range(4)
            ]
            left, right = one_hot_sum(terms, ids, block_count)
            lefts.append(left)
            rights.append(right)
        return total + nt_dot(jnp.concatenate(lefts, axis=1), jnp.concatenate(rights, axis=1))

    width = 4 * block_count
    total = lax.fori_loop(
        0, 4 * (elem_rows // group), gather_terms, jnp.zeros((SPLITS * width, BLOCK), jnp.float32)
    )
    total = sum(total[s * width : (s + 1) * width, :] for s in range(SPLITS))
    owned = 2 * owned_slots
    for c in range(4):
        own_ref[c * owned : (c + 1) * owned, :] = total[c * block_count : c * block_count + owned, :]
        for k in range(6):
            first = c * block_count + owned + 2 * k
            cut_ref[k, 2 * c : 2 * c + 2, :] = total[first : first + 2, :]
    send_pairs(cut_ref, back_ref, back_x_ref, back_y_ref, [(1, 0), (3, 2), (5, 4)])


def residual_kernel(counts, back_ref, far_x_ref, far_y_ref, own_ref, halos_ref, out_ref, came_ref):
    far_refs = [far_x_ref, far_y_ref if counts[1] > 2 else None, None]
    for axis, (place_at, inside, outside) in enumerate(arrivals(back_ref, far_refs, counts)):
        came_ref[2 * axis + place_at] = inside
        came_ref[2 * axis + 1 - place_at] = outside
    owned = own_ref.shape[0] // 4
    lefts, rights = [], []
    for k in range(6):
        parts = cut_parts(came_ref[k])
        for h in range(2):
            ids = halos_ref[2 * k + h : 2 * k + h + 1, :]
            terms = [parts[s][2 * c + h : 2 * c + h + 1, :] for s in range(SPLITS) for c in range(4)]
            left, right = one_hot_sum(terms, ids, owned)
            lefts.append(left)
            rights.append(right)
    total = nt_dot(jnp.concatenate(lefts, axis=1), jnp.concatenate(rights, axis=1))
    width = 4 * owned
    total = sum(total[s * width : (s + 1) * width, :] for s in range(SPLITS)) + own_ref[...]
    for c in range(4):
        for b in range(owned):
            r = c * owned + b
            out_ref[c : c + 1, b * BLOCK : (b + 1) * BLOCK] = total[r : r + 1, :]


def shaped(*shape):
    return jax.ShapeDtypeStruct(shape, jnp.float32)


def per_device(
    sizes,
    old_state,
    send_blocks,
    node_slots,
    node_weights,
    front_mask,
    halo_lists,
    elem_nodes,
    shape_grads,
    elem_volume,
):
    old_state, send_blocks = old_state[0, 0, 0], send_blocks[0, 0, 0]
    slots = send_blocks.shape[1]
    rows = FIELDS * slots
    old_rows = old_state.reshape(-1, BLOCK)
    swap, mine = pl.pallas_call(
        pack_far_kernel,
        out_shape=(shaped(2, rows, BLOCK), shaped(2, rows, BLOCK)),
        in_specs=[SMEM, VMEM],
        out_specs=(VMEM, VMEM),
        compiler_params=params(),
    )(send_blocks, old_rows)
    swap = lax.ppermute(swap, "layer", both_ways([(0, 1)]))
    near = pl.pallas_call(
        pack_near_kernel,
        out_shape=shaped(8, rows, BLOCK),
        in_specs=[SMEM, VMEM],
        out_specs=VMEM,
        compiler_params=params(),
    )(send_blocks, old_rows)
    near = group_swap(near, near_groups(sizes))
    first = lax.axis_index("layer") == 0
    pairs_two, pairs_one = far_pairs(sizes[0])
    sorted_far = [jnp.where(first, jnp.stack([mine[i], swap[i]]), jnp.stack([swap[i], mine[i]])) for i in range(2)]
    two = lax.ppermute(sorted_far[0], "mapx", pairs_two)
    one = lax.ppermute(sorted_far[1], "mapx", pairs_one)

    owned = node_slots.shape[-1]
    slot_rows = node_slots.reshape(-1, BLOCK)
    weight_rows = node_weights.reshape(-1, BLOCK)
    found = pl.pallas_call(
        near_kernel,
        out_shape=shaped(FIELDS, slot_rows.shape[0], BLOCK),
        in_specs=[VMEM, VMEM],
        out_specs=VMEM,
        compiler_params=params(),
    )(near, slot_rows)
    halo_rows = halo_lists.reshape(-1, BLOCK)
    halo_rows = jnp.pad(halo_rows, ((0, -halo_rows.shape[0] % 8), (0, 0)))
    chunk = (2 * FIELDS, BLOCK)
    new_state, table, group, far_x, far_y = pl.pallas_call(
        state_kernel,
        out_shape=(
            shaped(FIELDS, owned),
            shaped(owned // (2 * BLOCK), *chunk),
            shaped(8, *chunk),
            shaped(*chunk),
            shaped(*chunk),
        ),
        in_specs=[VMEM] * 7,
        out_specs=(VMEM,) * 5,
        scratch_shapes=[pltpu.VMEM((6, *chunk), jnp.float32)],
        compiler_params=params(),
    )(two, one, slot_rows, found, weight_rows, front_mask.reshape(-1, BLOCK), halo_rows)

    far_x = far_swap(far_x, "mapx", sizes[0])
    if sizes[1] > 2:
        far_y = far_swap(far_y, "mapy", sizes[1])
    group = group_swap(group, pair_groups(sizes))

    elems = elem_nodes.shape[-1]
    elem_rows = elems // BLOCK
    more = -elem_rows % 8
    nodes = jnp.pad(elem_nodes.reshape(4, elem_rows, BLOCK), ((0, 0), (0, more), (0, 0)))
    grads = jnp.pad(shape_grads.reshape(12, elem_rows, BLOCK), ((0, 0), (0, more), (0, 0)))
    volume = jnp.pad(elem_volume.reshape(elem_rows, BLOCK), ((0, more), (0, 0)))
    slots_all = table.shape[0] + 6
    own, back, back_x, back_y = pl.pallas_call(
        functools.partial(element_kernel, sizes, elem_rows),
        out_shape=(shaped(4 * owned // BLOCK, BLOCK), shaped(8, 8, BLOCK), shaped(8, BLOCK), shaped(8, BLOCK)),
        in_specs=[VMEM] * 7,
        out_specs=(VMEM,) * 4,
        scratch_shapes=[
            pltpu.VMEM((slots_all, *chunk), jnp.float32),
            pltpu.VMEM((4 * SPLITS, 4 * (elem_rows + more), BLOCK), jnp.float32),
            pltpu.VMEM((6, 8, BLOCK), jnp.float32),
        ],
        compiler_params=params(),
    )(table, group, far_x, far_y, nodes, grads, volume)

    back_x = far_swap(back_x, "mapx", sizes[0])
    if sizes[1] > 2:
        back_y = far_swap(back_y, "mapy", sizes[1])
    back = group_swap(back, pair_groups(sizes))
    residual = pl.pallas_call(
        functools.partial(residual_kernel, sizes),
        out_shape=shaped(4, owned),
        in_specs=[VMEM] * 5,
        out_specs=VMEM,
        scratch_shapes=[pltpu.VMEM((6, 8, BLOCK), jnp.float32)],
        compiler_params=params(),
    )(back, back_x, back_y, own, halo_rows)
    return (new_state[None, None, None], residual[None, None, None])


def solution(mesh):
    sizes = tuple(mesh.shape[axis] for axis in AXES)
    row = P("mapx", "mapy", "layer", None)
    table = P("mapx", "mapy", "layer", None, None)
    return jax.shard_map(
        functools.partial(per_device, sizes),
        mesh=mesh,
        in_specs=(table, table, table, table, row, table, table, table, row),
        out_specs=(table, table),
        check_vma=False,
    )
```

profile of v0, /device:TPU:18, one launch (start us, length us, event | category | flops | bytes accessed | tf_op | source)
XLA Modules:
  0.0 49.1 jit_solution(4717337641330893645)
XLA Ops:
  0.6 0.7 %copy.15 = s32[1,1,1,10,16]{4,3,2,1,0:T(8,128)S(1)} copy(s32[1,1,1,10,16]{4,2,3,1,0:T(1,128)} %param.10) | data formatting | bytes 1280
  1.3 0.9 %copy-done = f32[1,1,1,6,8192]{4,2,3,1,0:T(1,128)S(1)} copy-done((f32[1,1,1,6,8192]{4,2,3,1,0:T(1,128)S(1)}, f32[1,1,1,6,8192]{4,2,3,1,0:T(1,128)}, u32[]{:S(2)}) %copy-start) | copy-done | bytes 196632
  2.2 0.9 %shard_map.104 = (f32[2,96,128]{2,1,0:T(8,128)S(1)}, f32[2,96,128]{2,1,0:T(8,128)S(1)}) custom-call(s32[10,16]{1,0:T(8,128)S(1)} %bitcast.10, f32[384,128]{1,0:T(8,128)S(1)} %bitcast.8), custom_call_target="tpu_custom_call" | custom-call | tf_op jit(solution)/shard_map/pallas_call | solution.py:394
  3.1 0.1 collective-permute-start
  3.2 2.0 %shard_map.105 = f32[8,96,128]{2,1,0:T(8,128)} custom-call(s32[10,16]{1,0:T(8,128)S(1)} %bitcast.11, f32[384,128]{1,0:T(8,128)S(1)} %bitcast.9), custom_call_target="tpu_custom_call" | custom-call | tf_op jit(solution)/shard_map/pallas_call | solution.py:402
  5.2 4.3 %all-to-all-start = ((f32[8,96,128]{2,1,0:T(8,128)}), f32[8,96,128]{2,1,0:T(8,128)S(1)}, u32[]{:S(2)}, u32[]{:S(2)}) async-start(f32[8,96,128]{2,1,0:T(8,128)} %shard_map.105), calls=%async_computation | async-start | bytes 786432 | tf_op jit(solution)/shard_map/all_to_all | solution.py:59
  9.6 0.7 %collective-permute-start.2 = (f32[2,96,128]{2,1,0:T(8,128)S(1)}, f32[2,96,128]{2,1,0:T(8,128)S(1)}, u32[]{:S(2)}, u32[]{:S(2)}) collective-permute-start(f32[2,96,128]{2,1,0:T(8,128)S(1)} %maximum_select_fusion.1), channel_id=1, source_target_pairs={{12,16},{16,12},{13,17},{17,13},{14,18},{18,14},{15,19},{19,15}} | collective-permute-start | bytes 294920 | tf_op jit(solution)/shard_map/ppermute | solution.py:414
  10.3 0.0 copy-start.5
  10.3 0.0 copy-start.7
  10.3 4.6 %collective-permute-start.1 = (f32[2,96,128]{2,1,0:T(8,128)S(1)}, f32[2,96,128]{2,1,0:T(8,128)S(1)}, u32[]{:S(2)}, u32[]{:S(2)}) collective-permute-start(f32[2,96,128]{2,1,0:T(8,128)S(1)} %maximum_select_fusion), channel_id=1, source_target_pairs={{8,16},{16,8},{12,20},{20,12},{9,17},{17,9},{13,21},{21,13},{10,18... | collective-permute-start | bytes 294920 | tf_op jit(solution)/shard_map/ppermute | solution.py:413
  15.0 0.0 copy-start.6
  15.0 0.7 %copy-done.6 = f32[1,1,1,4,512]{4,3,2,1,0:T(4,128)S(1)} copy-done((f32[1,1,1,4,512]{4,3,2,1,0:T(4,128)S(1)}, f32[1,1,1,4,512]{4,3,2,1,0:T(4,128)}, u32[]{:S(2)}) %copy-start.6) | copy-done | bytes 8216
  15.7 1.0 %all-to-all-done.near_ref = f32[8,96,128]{2,1,0:T(8,128)S(1)} async-done(((f32[8,96,128]{2,1,0:T(8,128)}), f32[8,96,128]{2,1,0:T(8,128)S(1)}, u32[]{:S(2)}, u32[]{:S(2)}) %all-to-all-start) | async-done | bytes 393248 | tf_op jit(solution)/shard_map/all_to_all | solution.py:59
  16.7 2.2 %shard_map.106.found_ref = f32[6,16,128]{2,1,0:T(8,128)S(1)} custom-call(f32[8,96,128]{2,1,0:T(8,128)S(1)} %all-to-all-done.near_ref, s32[16,128]{1,0:T(8,128)S(1)} %reshape.25.slots_ref), custom_call_target="tpu_custom_call" | custom-call | tf_op jit(solution)/shard_map/pallas_call | solution.py:419
  19.0 0.0 collective-permute-done.1.two_ref
  19.0 1.9 %shard_map.107 = (f32[6,512]{1,0:T(8,128)S(1)}, f32[2,12,128]{2,1,0:T(8,128)S(1)}, f32[8,12,128]{2,1,0:T(8,128)}, f32[12,128]{1,0:T(8,128)S(1)}, f32[12,128]{1,0:T(8,128)S(1)}) custom-call(f32[2,96,128]{2,1,0:T(8,128)S(1)} %collective-permute-done.1.two_ref, f32[2,96,128]{2,1,0:T(8,128)S(1)} %collective-permute-done.2.one_ref, ...), custom_call_target="tpu_custom_call" | custom-call | tf_op jit(solution)/shard_map/pallas_call | solution.py:429
  20.9 5.7 %all-to-all-start.1 = ((f32[8,12,128]{2,1,0:T(8,128)}), f32[8,12,128]{2,1,0:T(8,128)S(1)}, u32[]{:S(2)}, u32[]{:S(2)}) async-start(f32[8,12,128]{2,1,0:T(8,128)} %get-tuple-element.17), calls=%async_computation.1 | async-start | bytes 131072 | tf_op jit(solution)/shard_map/all_to_all | solution.py:59
  26.6 1.9 %collective-permute-start.3 = (f32[12,128]{1,0:T(8,128)S(1)}, f32[12,128]{1,0:T(8,128)S(1)}, u32[]{:S(2)}, u32[]{:S(2)}) collective-permute-start(f32[12,128]{1,0:T(8,128)S(1)} %get-tuple-element.18), channel_id=1, source_target_pairs={{4,8},{8,4},{12,16},{16,12},{20,24},{24,20},{5,9},{9,5},{13,17},{1... | collective-permute-start | bytes 18440 | tf_op jit(solution)/shard_map/ppermute | solution.py:66
  28.6 0.3 reduce.1
  28.9 0.0 copy-start.3
  28.9 0.7 %copy-done.3 = s32[1,1,1,4,2560]{4,3,2,1,0:T(4,128)S(1)} copy-done((s32[1,1,1,4,2560]{4,3,2,1,0:T(4,128)S(1)}, s32[1,1,1,4,2560]{4,3,2,1,0:T(4,128)}, u32[]{:S(2)}) %copy-start.3) | copy-done | bytes 40984
  29.7 0.0 copy-start.4
  29.7 0.7 %copy-done.4 = f32[1,1,1,2560]{3,2,1,0:T(1,128)S(1)} copy-done((f32[1,1,1,2560]{3,2,1,0:T(1,128)S(1)}, f32[1,1,1,2560]{3,2,1,0:T(1,128)}, u32[]{:S(2)}) %copy-start.4) | copy-done | bytes 10264
  30.4 2.6 %collective-permute-done.3.far_x_ref = f32[12,128]{1,0:T(8,128)S(1)} collective-permute-done((f32[12,128]{1,0:T(8,128)S(1)}, f32[12,128]{1,0:T(8,128)S(1)}, u32[]{:S(2)}, u32[]{:S(2)}) %collective-permute-start.3) | collective-permute-done | bytes 6176 | tf_op jit(solution)/shard_map/ppermute | solution.py:66
  33.1 0.0 all-to-all-done.1.group_ref
  33.1 4.6 %shard_map.108 = (f32[16,128]{1,0:T(8,128)S(1)}, f32[8,8,128]{2,1,0:T(8,128)}, f32[8,128]{1,0:T(8,128)S(1)}, f32[8,128]{1,0:T(8,128)S(1)}) custom-call(f32[2,12,128]{2,1,0:T(8,128)S(1)} %get-tuple-element.16.table_in_ref, f32[8,12,128]{2,1,0:T(8,128)S(1)} %all-to-all-done.1.group_ref, f32[12,128]{1,0:T(8,128)S(1)} %collective-permute-done.3.far_x_ref, ...), custom_call_target="tpu_custom_call" | custom-call | tf_op jit(solution)/shard_map/pallas_call | solution.py:456
  37.6 4.2 %all-to-all-start.2 = ((f32[8,8,128]{2,1,0:T(8,128)}), f32[8,8,128]{2,1,0:T(8,128)S(1)}, u32[]{:S(2)}, u32[]{:S(2)}) async-start(f32[8,8,128]{2,1,0:T(8,128)} %get-tuple-element.20), calls=%async_computation.2 | async-start | bytes 65536 | tf_op jit(solution)/shard_map/all_to_all | solution.py:59
  41.8 1.9 %collective-permute-start.4 = (f32[8,128]{1,0:T(8,128)S(1)}, f32[8,128]{1,0:T(8,128)S(1)}, u32[]{:S(2)}, u32[]{:S(2)}) collective-permute-start(f32[8,128]{1,0:T(8,128)S(1)} %get-tuple-element.21), channel_id=1, source_target_pairs={{4,8},{8,4},{12,16},{16,12},{20,24},{24,20},{5,9},{9,5},{13,17},{1... | collective-permute-start | bytes 12296 | tf_op jit(solution)/shard_map/ppermute | solution.py:66
  43.8 0.6 %copy.12 = f32[1,1,1,6,512]{4,2,3,1,0:T(1,128)} copy(f32[1,1,1,6,512]{4,3,2,1,0:T(8,128)S(1)} %bitcast.12) | data formatting | bytes 24576
  44.4 3.9 %collective-permute-done.4.far_x_ref = f32[8,128]{1,0:T(8,128)S(1)} collective-permute-done((f32[8,128]{1,0:T(8,128)S(1)}, f32[8,128]{1,0:T(8,128)S(1)}, u32[]{:S(2)}, u32[]{:S(2)}) %collective-permute-start.4) | collective-permute-done | bytes 4128 | tf_op jit(solution)/shard_map/ppermute | solution.py:66
  48.2 0.0 all-to-all-done.2.back_ref
  48.2 0.9 %shard_map.109 = f32[4,512]{1,0:T(4,128)} custom-call(f32[8,8,128]{2,1,0:T(8,128)S(1)} %all-to-all-done.2.back_ref, f32[8,128]{1,0:T(8,128)S(1)} %collective-permute-done.4.far_x_ref, f32[8,128]{1,0:T(8,128)S(1)} %get-tuple-element.22.far_y_ref, f32[16,128]{1,0:T(8,128)S(1)} %get-tuple-element.23.own_ref, s32[16,128]{1,0:T(8,128)S(1)} %pad.16.halos_ref), custom_call_target="tpu_custom_call" | custom-call | tf_op jit(solution)/shard_map/pallas_call | solution.py:473
  (24 shorter events, 0.2 us)
Async XLA Ops:
  1.3 0.9 %copy-start = (f32[1,1,1,6,8192]{4,2,3,1,0:T(1,128)S(1)}, f32[1,1,1,6,8192]{4,2,3,1,0:T(1,128)}, u32[]{:S(2)}) copy-start(f32[1,1,1,6,8192]{4,2,3,1,0:T(1,128)} %param.9) | copy-start | bytes 589828
  3.1 6.4 %collective-permute-start = (f32[2,96,128]{2,1,0:T(8,128)S(1)}, f32[2,96,128]{2,1,0:T(8,128)S(1)}, u32[]{:S(2)}, u32[]{:S(2)}) collective-permute-start(f32[2,96,128]{2,1,0:T(8,128)S(1)} %get-tuple-element.14), channel_id=1, source_target_pairs={{0,1},{1,0},{2,3},{3,2},{4,5},{5,4},{6,7},{7,6},{8,9},{9,8},{10,11... | collective-permute-start | bytes 294920 | tf_op jit(solution)/shard_map/ppermute | solution.py:401
  5.2 11.5 %all-to-all-start = ((f32[8,96,128]{2,1,0:T(8,128)}), f32[8,96,128]{2,1,0:T(8,128)S(1)}, u32[]{:S(2)}, u32[]{:S(2)}) async-start(f32[8,96,128]{2,1,0:T(8,128)} %shard_map.105), calls=%async_computation | async-start | bytes 786432 | tf_op jit(solution)/shard_map/all_to_all | solution.py:59
  9.6 9.4 %collective-permute-start.2 = (f32[2,96,128]{2,1,0:T(8,128)S(1)}, f32[2,96,128]{2,1,0:T(8,128)S(1)}, u32[]{:S(2)}, u32[]{:S(2)}) collective-permute-start(f32[2,96,128]{2,1,0:T(8,128)S(1)} %maximum_select_fusion.1), channel_id=1, source_target_pairs={{12,16},{16,12},{13,17},{17,13},{14,18},{18,14},{15,19},{19,15}} | collective-permute-start | bytes 294920 | tf_op jit(solution)/shard_map/ppermute | solution.py:414
  10.3 4.7 %copy-start.5 = (s32[1,1,1,4,512]{4,3,2,1,0:T(4,128)S(1)}, s32[1,1,1,4,512]{4,3,2,1,0:T(4,128)}, u32[]{:S(2)}) copy-start(s32[1,1,1,4,512]{4,3,2,1,0:T(4,128)} %param.11) | copy-start | bytes 24580
  10.3 4.7 %copy-start.7 = (s32[1,1,1,6,256]{4,2,3,1,0:T(1,128)S(1)}, s32[1,1,1,6,256]{4,2,3,1,0:T(1,128)}, u32[]{:S(2)}) copy-start(s32[1,1,1,6,256]{4,2,3,1,0:T(1,128)} %param.14) | copy-start | bytes 18436
  10.3 8.7 %collective-permute-start.1 = (f32[2,96,128]{2,1,0:T(8,128)S(1)}, f32[2,96,128]{2,1,0:T(8,128)S(1)}, u32[]{:S(2)}, u32[]{:S(2)}) collective-permute-start(f32[2,96,128]{2,1,0:T(8,128)S(1)} %maximum_select_fusion), channel_id=1, source_target_pairs={{8,16},{16,8},{12,20},{20,12},{9,17},{17,9},{13,21},{21,13},{10,18... | collective-permute-start | bytes 294920 | tf_op jit(solution)/shard_map/ppermute | solution.py:413
  15.0 0.7 %copy-start.6 = (f32[1,1,1,4,512]{4,3,2,1,0:T(4,128)S(1)}, f32[1,1,1,4,512]{4,3,2,1,0:T(4,128)}, u32[]{:S(2)}) copy-start(f32[1,1,1,4,512]{4,3,2,1,0:T(4,128)} %param.12) | copy-start | bytes 24580
  16.7 2.3 %copy-start.1 = (s32[1,1,1,512]{3,2,1,0:T(1,128)S(1)}, s32[1,1,1,512]{3,2,1,0:T(1,128)}, u32[]{:S(2)}) copy-start(s32[1,1,1,512]{3,2,1,0:T(1,128)} %param.13) | copy-start | bytes 6148
  20.9 7.7 %copy-start.2 = (f32[1,1,1,12,2560]{4,2,3,1,0:T(1,128)S(1)}, f32[1,1,1,12,2560]{4,2,3,1,0:T(1,128)}, u32[]{:S(2)}) copy-start(f32[1,1,1,12,2560]{4,2,3,1,0:T(1,128)} %param.16) | copy-start | bytes 368644
  20.9 12.2 %all-to-all-start.1 = ((f32[8,12,128]{2,1,0:T(8,128)}), f32[8,12,128]{2,1,0:T(8,128)S(1)}, u32[]{:S(2)}, u32[]{:S(2)}) async-start(f32[8,12,128]{2,1,0:T(8,128)} %get-tuple-element.17), calls=%async_computation.1 | async-start | bytes 131072 | tf_op jit(solution)/shard_map/all_to_all | solution.py:59
  26.6 6.4 %collective-permute-start.3 = (f32[12,128]{1,0:T(8,128)S(1)}, f32[12,128]{1,0:T(8,128)S(1)}, u32[]{:S(2)}, u32[]{:S(2)}) collective-permute-start(f32[12,128]{1,0:T(8,128)S(1)} %get-tuple-element.18), channel_id=1, source_target_pairs={{4,8},{8,4},{12,16},{16,12},{20,24},{24,20},{5,9},{9,5},{13,17},{1... | collective-permute-start | bytes 18440 | tf_op jit(solution)/shard_map/ppermute | solution.py:66
  28.9 0.8 %copy-start.3 = (s32[1,1,1,4,2560]{4,3,2,1,0:T(4,128)S(1)}, s32[1,1,1,4,2560]{4,3,2,1,0:T(4,128)}, u32[]{:S(2)}) copy-start(s32[1,1,1,4,2560]{4,3,2,1,0:T(4,128)} %param.15) | copy-start | bytes 122884
  29.7 0.7 %copy-start.4 = (f32[1,1,1,2560]{3,2,1,0:T(1,128)S(1)}, f32[1,1,1,2560]{3,2,1,0:T(1,128)}, u32[]{:S(2)}) copy-start(f32[1,1,1,2560]{3,2,1,0:T(1,128)} %param.17) | copy-start | bytes 30724
  37.6 10.6 %all-to-all-start.2 = ((f32[8,8,128]{2,1,0:T(8,128)}), f32[8,8,128]{2,1,0:T(8,128)S(1)}, u32[]{:S(2)}, u32[]{:S(2)}) async-start(f32[8,8,128]{2,1,0:T(8,128)} %get-tuple-element.20), calls=%async_computation.2 | async-start | bytes 65536 | tf_op jit(solution)/shard_map/all_to_all | solution.py:59
  41.8 6.4 %collective-permute-start.4 = (f32[8,128]{1,0:T(8,128)S(1)}, f32[8,128]{1,0:T(8,128)S(1)}, u32[]{:S(2)}, u32[]{:S(2)}) collective-permute-start(f32[8,128]{1,0:T(8,128)S(1)} %get-tuple-element.21), channel_id=1, source_target_pairs={{4,8},{8,4},{12,16},{16,12},{20,24},{24,20},{5,9},{9,5},{13,17},{1... | collective-permute-start | bytes 12296 | tf_op jit(solution)/shard_map/ppermute | solution.py:66
where the time goes:
time: 49.8 us; the launch traced here: 49.1 us
  starting transfers between devices  23.4 us (47%)
  Pallas kernels  12.5 us (25%)
  waiting for transfers between devices  7.54 us (15%)
  local copies, waits for them, and re-layouts  4.46 us (9%)
  between operations  0.87 us (2%)
    all_to_all x3, starting transfers between devices, group_swap(): lax.all_to_all(chunks, AXES, split_axis=0, concat_axis=0, axis_index_grou...  14.3 us
    ppermute x2, waiting for transfers between devices, far_swap(): return lax.ppermute(value, axis, pairs)  6.49 us
    ppermute x1, starting transfers between devices, per_device(): two = lax.ppermute(sorted_far[0], 'mapx', pairs_two)  4.62 us
    pallas_call x1, Pallas kernels, per_device(): pl.pallas_call(functools.partial(element_kernel, sizes, elem_rows), out_s...  4.55 us
    unnamed x18, local copies, waits for them, and re-layouts  4.36 us
    ppermute x2, starting transfers between devices, far_swap(): return lax.ppermute(value, axis, pairs)  3.82 us
    pallas_call x1, Pallas kernels, per_device(): pl.pallas_call(near_kernel, out_shape=shaped(FIELDS, slot_rows.shape[0],...  2.23 us
    pallas_call x1, Pallas kernels, per_device(): pl.pallas_call(pack_near_kernel, out_shape=shaped(8, rows, BLOCK), in_spe...  2 us
  transfers between devices with their start and end apart: 8, of which 3 were waited for; matrix products, arithmetic and copies ran while one was open for 2% of the time, Pallas kernels for 9%

commit v1 on v0

--- a/solution.py
+++ b/solution.py
@@ -55,6 +55,10 @@
     ]
 
 
+def group_gather(portions, groups):
+    return lax.all_gather(portions, AXES, axis_index_groups=groups)
+
+
 def group_swap(chunks, groups):
     return lax.all_to_all(chunks, AXES, split_axis=0, concat_axis=0, axis_index_groups=groups)
 
@@ -67,10 +71,10 @@
 
 
 def put_blocks(blocks_ref, old_ref, out_ref, chunk, peer):
-    slots = blocks_ref.shape[1]
+    slots = blocks_ref.shape[2]
     count = old_ref.shape[0] // FIELDS
     for c in range(slots):
-        rows = pl.ds(blocks_ref[peer, c], FIELDS, stride=count)
+        rows = pl.ds(blocks_ref[peer, 0, c], FIELDS, stride=count)
         out_ref[chunk, FIELDS * c : FIELDS * (c + 1), :] = old_ref[rows, :]
 
 
@@ -205,7 +209,7 @@
         even, odd = order[axis]
         inside = jnp.where(places[axis] == 0, even, odd)
         outside = jnp.where(places[axis] == 0, odd, even)
-        group_ref[partner(*places, axis)] = cut_ref[inside]
+        group_ref[axis] = cut_ref[inside]
         if axis == 0:
             far_x_ref[...] = cut_ref[outside]
         if axis == 1:
@@ -216,7 +220,7 @@
     places = pair_places()
     result = []
     for axis in range(3):
-        inside = group_ref[partner(*places, axis)]
+        inside = group_ref[partner(*places, axis), axis]
         at = lax.axis_index(AXES[axis])
         edge = jnp.where(places[axis] == 0, at == 0, at == counts[axis] - 1)
         if far_refs[axis] is None:
@@ -389,6 +393,7 @@
 ):
     old_state, send_blocks = old_state[0, 0, 0], send_blocks[0, 0, 0]
     slots = send_blocks.shape[1]
+    send_blocks = send_blocks.reshape(-1, 1, slots)
     rows = FIELDS * slots
     old_rows = old_state.reshape(-1, BLOCK)
     swap, mine = pl.pallas_call(
@@ -431,7 +436,7 @@
         out_shape=(
             shaped(FIELDS, owned),
             shaped(owned // (2 * BLOCK), *chunk),
-            shaped(8, *chunk),
+            shaped(3, *chunk),
             shaped(*chunk),
             shaped(*chunk),
         ),
@@ -444,7 +449,7 @@
     far_x = far_swap(far_x, "mapx", sizes[0])
     if sizes[1] > 2:
         far_y = far_swap(far_y, "mapy", sizes[1])
-    group = group_swap(group, pair_groups(sizes))
+    group = group_gather(group, pair_groups(sizes))
 
     elems = elem_nodes.shape[-1]
     elem_rows = elems // BLOCK
@@ -455,7 +460,7 @@
     slots_all = table.shape[0] + 6
     own, back, back_x, back_y = pl.pallas_call(
         functools.partial(element_kernel, sizes, elem_rows),
-        out_shape=(shaped(4 * owned // BLOCK, BLOCK), shaped(8, 8, BLOCK), shaped(8, BLOCK), shaped(8, BLOCK)),
+        out_shape=(shaped(4 * owned // BLOCK, BLOCK), shaped(3, 8, BLOCK), shaped(8, BLOCK), shaped(8, BLOCK)),
         in_specs=[VMEM] * 7,
         out_specs=(VMEM,) * 4,
         scratch_shapes=[
@@ -469,7 +474,7 @@
     back_x = far_swap(back_x, "mapx", sizes[0])
     if sizes[1] > 2:
         back_y = far_swap(back_y, "mapy", sizes[1])
-    back = group_swap(back, pair_groups(sizes))
+    back = group_gather(back, pair_groups(sizes))
     residual = pl.pallas_call(
         functools.partial(residual_kernel, sizes),
         out_shape=shaped(4, owned),

time: 49.8 us -> 54.7 us (1.098)
  the two profiles are of different devices: /device:TPU:18 before, /device:TPU:0 now
where the time goes in v1:
time: 54.7 us; the launch traced here: 54.2 us
  blocking collectives  26.1 us (48%)
  Pallas kernels  11 us (20%)
  starting transfers between devices  8.2 us (15%)
  local copies, waits for them, and re-layouts  4.46 us (8%)
  waiting for transfers between devices  3.25 us (6%)
  between operations  0.89 us (2%)
    all_gather x2, blocking collectives, group_gather(): return lax.all_gather(portions, AXES, axis_index_groups=groups)  26.1 us
    all_to_all x1, starting transfers between devices, group_swap(): lax.all_to_all(chunks, AXES, split_axis=0, concat_axis=0, axis_index_grou...  4.89 us
    unnamed x19, local copies, waits for them, and re-layouts  4.35 us
    pallas_call x1, Pallas kernels, per_device(): pl.pallas_call(functools.partial(element_kernel, sizes, elem_rows), out_s...  3.88 us
    all_to_all x1, waiting for transfers between devices, group_swap(): lax.all_to_all(chunks, AXES, split_axis=0, concat_axis=0, axis_index_grou...  3.23 us
    pallas_call x1, Pallas kernels, per_device(): pl.pallas_call(near_kernel, out_shape=shaped(FIELDS, slot_rows.shape[0],...  2.23 us
    pallas_call x1, Pallas kernels, per_device(): pl.pallas_call(pack_near_kernel, out_shape=shaped(8, rows, BLOCK), in_spe...  1.84 us
    ppermute x2, starting transfers between devices, far_swap(): return lax.ppermute(value, axis, pairs)  1.32 us
  transfers between devices with their start and end apart: 6, of which 1 were waited for; matrix products, arithmetic and copies ran while one was open for 2% of the time, Pallas kernels for 8%

profile of v1, /device:TPU:0, one launch (start us, length us, event | category | flops | bytes accessed | tf_op | source)
XLA Modules:
  0.0 54.2 jit_solution(9665020950846746460)
XLA Ops:
  0.6 0.9 %copy-done = f32[1,1,1,6,8192]{4,2,3,1,0:T(1,128)S(1)} copy-done((f32[1,1,1,6,8192]{4,2,3,1,0:T(1,128)S(1)}, f32[1,1,1,6,8192]{4,2,3,1,0:T(1,128)}, u32[]{:S(2)}) %copy-start) | copy-done | bytes 196632
  1.6 0.7 %copy-done.1 = s32[1,1,1,10,16]{4,2,3,1,0:T(1,128)S(1)} copy-done((s32[1,1,1,10,16]{4,2,3,1,0:T(1,128)S(1)}, s32[1,1,1,10,16]{4,2,3,1,0:T(1,128)}, u32[]{:S(2)}) %copy-start.1) | copy-done | bytes 664
  2.2 0.8 %shard_map.104 = (f32[2,96,128]{2,1,0:T(8,128)S(1)}, f32[2,96,128]{2,1,0:T(8,128)S(1)}) custom-call(s32[10,1,16]{2,1,0:T(1,128)S(1)} %bitcast.12, f32[384,128]{1,0:T(8,128)S(1)} %bitcast.9), custom_call_target="tpu_custom_call" | custom-call | tf_op jit(solution)/shard_map/pallas_call | solution.py:399
  3.1 0.5 collective-permute-start
  3.6 1.8 %shard_map.105 = f32[8,96,128]{2,1,0:T(8,128)} custom-call(s32[10,1,16]{2,1,0:T(1,128)S(1)} %bitcast.13, f32[384,128]{1,0:T(8,128)S(1)} %bitcast.10), custom_call_target="tpu_custom_call" | custom-call | tf_op jit(solution)/shard_map/pallas_call | solution.py:407
  5.5 4.9 %all-to-all-start = ((f32[8,96,128]{2,1,0:T(8,128)}), f32[8,96,128]{2,1,0:T(8,128)S(1)}, u32[]{:S(2)}, u32[]{:S(2)}) async-start(f32[8,96,128]{2,1,0:T(8,128)} %shard_map.105), calls=%async_computation | async-start | bytes 786432 | tf_op jit(solution)/shard_map/all_to_all | solution.py:63
  10.4 0.0 collective-permute-done
  10.4 0.7 %collective-permute-start.2 = (f32[2,96,128]{2,1,0:T(8,128)S(1)}, f32[2,96,128]{2,1,0:T(8,128)S(1)}, u32[]{:S(2)}, u32[]{:S(2)}) collective-permute-start(f32[2,96,128]{2,1,0:T(8,128)S(1)} %maximum_select_fusion.1), channel_id=1, source_target_pairs={{12,16},{16,12},{13,17},{17,13},{14,18},{18,14},{15,19},{19,15}} | collective-permute-start | bytes 294920 | tf_op jit(solution)/shard_map/ppermute | solution.py:419
  11.1 0.0 copy-start.6
  11.1 0.0 copy-start.3
  11.1 0.0 copy-start.8
  11.1 0.8 %collective-permute-start.1 = (f32[2,96,128]{2,1,0:T(8,128)S(1)}, f32[2,96,128]{2,1,0:T(8,128)S(1)}, u32[]{:S(2)}, u32[]{:S(2)}) collective-permute-start(f32[2,96,128]{2,1,0:T(8,128)S(1)} %maximum_select_fusion), channel_id=1, source_target_pairs={{8,16},{16,8},{12,20},{20,12},{9,17},{17,9},{13,21},{21,13},{10,18... | collective-permute-start | bytes 294920 | tf_op jit(solution)/shard_map/ppermute | solution.py:418
  12.0 0.0 copy-start.7
  12.0 0.7 %copy-done.7 = f32[1,1,1,4,512]{4,3,2,1,0:T(4,128)S(1)} copy-done((f32[1,1,1,4,512]{4,3,2,1,0:T(4,128)S(1)}, f32[1,1,1,4,512]{4,3,2,1,0:T(4,128)}, u32[]{:S(2)}) %copy-start.7) | copy-done | bytes 8216
  12.7 0.3 reduce.1
  13.0 0.0 copy-start.4
  13.1 0.7 %copy-done.4 = s32[1,1,1,4,2560]{4,3,2,1,0:T(4,128)S(1)} copy-done((s32[1,1,1,4,2560]{4,3,2,1,0:T(4,128)S(1)}, s32[1,1,1,4,2560]{4,3,2,1,0:T(4,128)}, u32[]{:S(2)}) %copy-start.4) | copy-done | bytes 40984
  13.8 0.0 copy-start.5
  13.8 0.7 %copy-done.5 = f32[1,1,1,2560]{3,2,1,0:T(1,128)S(1)} copy-done((f32[1,1,1,2560]{3,2,1,0:T(1,128)S(1)}, f32[1,1,1,2560]{3,2,1,0:T(1,128)}, u32[]{:S(2)}) %copy-start.5) | copy-done | bytes 10264
  14.6 3.2 %all-to-all-done.near_ref = f32[8,96,128]{2,1,0:T(8,128)S(1)} async-done(((f32[8,96,128]{2,1,0:T(8,128)}), f32[8,96,128]{2,1,0:T(8,128)S(1)}, u32[]{:S(2)}, u32[]{:S(2)}) %all-to-all-start) | async-done | bytes 393248 | tf_op jit(solution)/shard_map/all_to_all | solution.py:63
  17.8 2.2 %shard_map.106.found_ref = f32[6,16,128]{2,1,0:T(8,128)S(1)} custom-call(f32[8,96,128]{2,1,0:T(8,128)S(1)} %all-to-all-done.near_ref, s32[16,128]{1,0:T(8,128)S(1)} %reshape.25.slots_ref), custom_call_target="tpu_custom_call" | custom-call | tf_op jit(solution)/shard_map/pallas_call | solution.py:424
  20.1 0.0 collective-permute-done.2.one_ref
  20.1 0.0 collective-permute-done.1.two_ref
  20.1 1.3 %shard_map.107 = (f32[6,512]{1,0:T(8,128)S(1)}, f32[2,12,128]{2,1,0:T(8,128)S(1)}, f32[3,12,128]{2,1,0:T(8,128)S(1)}, f32[12,128]{1,0:T(8,128)S(1)}, f32[12,128]{1,0:T(8,128)S(1)}) custom-call(f32[2,96,128]{2,1,0:T(8,128)S(1)} %collective-permute-done.1.two_ref, f32[2,96,128]{2,1,0:T(8,128)S(1)} %collective-permute-done.2.one_ref, ...), custom_call_target="tpu_custom_call" | custom-call | tf_op jit(solution)/shard_map/pallas_call | solution.py:434
  21.4 0.7 %collective-permute-start.3 = (f32[12,128]{1,0:T(8,128)S(1)}, f32[12,128]{1,0:T(8,128)S(1)}, u32[]{:S(2)}, u32[]{:S(2)}) collective-permute-start(f32[12,128]{1,0:T(8,128)S(1)} %get-tuple-element.18), channel_id=1, source_target_pairs={{4,8},{8,4},{12,16},{16,12},{20,24},{24,20},{5,9},{9,5},{13,17},{1... | collective-permute-start | bytes 18440 | tf_op jit(solution)/shard_map/ppermute | solution.py:70
  22.0 14.7 %all-gather = f32[24,12,128]{2,1,0:T(8,128)S(1)} all-gather(f32[3,12,128]{2,1,0:T(8,128)S(1)} %get-tuple-element.17), channel_id=2, replica_groups={{0,1,2,3,4,5,6,7},{8,9,10,11,12,13,14,15},{16,17,18,19,20,21,22,23},{24..., dimensions={0}, use_global_device_ids=true | all-gather | bytes 165888 | tf_op jit(solution)/shard_map/all_gather | solution.py:59
  36.7 0.6 %copy.13 = f32[1,1,1,6,512]{4,2,3,1,0:T(1,128)} copy(f32[1,1,1,6,512]{4,3,2,1,0:T(8,128)S(1)} %bitcast.14) | data formatting | bytes 24576
  37.3 3.9 %shard_map.108 = (f32[16,128]{1,0:T(8,128)S(1)}, f32[3,8,128]{2,1,0:T(8,128)S(1)}, f32[8,128]{1,0:T(8,128)S(1)}, f32[8,128]{1,0:T(8,128)S(1)}) custom-call(f32[2,12,128]{2,1,0:T(8,128)S(1)} %get-tuple-element.16.table_in_ref, f32[8,3,12,128]{3,2,1,0:T(8,128)S(1)} %bitcast.8, f32[12,128]{1,0:T(8,128)S(1)} %collective-permute-done.3.far_x_ref, ...), custom_call_target="tpu_custom_call" | custom-call | tf_op jit(solution)/shard_map/pallas_call | solution.py:461
  41.2 0.7 %collective-permute-start.4 = (f32[8,128]{1,0:T(8,128)S(1)}, f32[8,128]{1,0:T(8,128)S(1)}, u32[]{:S(2)}, u32[]{:S(2)}) collective-permute-start(f32[8,128]{1,0:T(8,128)S(1)} %get-tuple-element.21), channel_id=1, source_target_pairs={{4,8},{8,4},{12,16},{16,12},{20,24},{24,20},{5,9},{9,5},{13,17},{1... | collective-permute-start | bytes 12296 | tf_op jit(solution)/shard_map/ppermute | solution.py:70
  41.9 11.4 %all-gather.1 = f32[24,8,128]{2,1,0:T(8,128)S(1)} all-gather(f32[3,8,128]{2,1,0:T(8,128)S(1)} %get-tuple-element.20), channel_id=3, replica_groups={{0,1,2,3,4,5,6,7},{8,9,10,11,12,13,14,15},{16,17,18,19,20,21,22,23},{24..., dimensions={0}, use_global_device_ids=true | all-gather | bytes 110592 | tf_op jit(solution)/shard_map/all_gather | solution.py:59
  53.3 0.0 collective-permute-done.4.far_x_ref
  53.3 0.9 %shard_map.109 = f32[4,512]{1,0:T(4,128)} custom-call(f32[8,3,8,128]{3,2,1,0:T(8,128)S(1)} %bitcast.11, f32[8,128]{1,0:T(8,128)S(1)} %collective-permute-done.4.far_x_ref, f32[8,128]{1,0:T(8,128)S(1)} %get-tuple-element.22.far_y_ref, f32[16,128]{1,0:T(8,128)S(1)} %get-tuple-element.23.own_ref, s32[16,128]{1,0:T(8,128)S(1)} %pad.16.halos_ref), custom_call_target="tpu_custom_call" | custom-call | tf_op jit(solution)/shard_map/pallas_call | solution.py:478
  (23 shorter events, 0.2 us)
Async XLA Ops:
  0.6 0.9 %copy-start = (f32[1,1,1,6,8192]{4,2,3,1,0:T(1,128)S(1)}, f32[1,1,1,6,8192]{4,2,3,1,0:T(1,128)}, u32[]{:S(2)}) copy-start(f32[1,1,1,6,8192]{4,2,3,1,0:T(1,128)} %param.9) | copy-start | bytes 589828
  1.6 0.7 %copy-start.1 = (s32[1,1,1,10,16]{4,2,3,1,0:T(1,128)S(1)}, s32[1,1,1,10,16]{4,2,3,1,0:T(1,128)}, u32[]{:S(2)}) copy-start(s32[1,1,1,10,16]{4,2,3,1,0:T(1,128)} %param.10) | copy-start | bytes 1924
  3.1 7.3 %collective-permute-start = (f32[2,96,128]{2,1,0:T(8,128)S(1)}, f32[2,96,128]{2,1,0:T(8,128)S(1)}, u32[]{:S(2)}, u32[]{:S(2)}) collective-permute-start(f32[2,96,128]{2,1,0:T(8,128)S(1)} %get-tuple-element.14), channel_id=1, source_target_pairs={{0,1},{1,0},{2,3},{3,2},{4,5},{5,4},{6,7},{7,6},{8,9},{9,8},{10,11... | collective-permute-start | bytes 294920 | tf_op jit(solution)/shard_map/ppermute | solution.py:406
  5.5 12.4 %all-to-all-start = ((f32[8,96,128]{2,1,0:T(8,128)}), f32[8,96,128]{2,1,0:T(8,128)S(1)}, u32[]{:S(2)}, u32[]{:S(2)}) async-start(f32[8,96,128]{2,1,0:T(8,128)} %shard_map.105), calls=%async_computation | async-start | bytes 786432 | tf_op jit(solution)/shard_map/all_to_all | solution.py:63
  10.4 9.7 %collective-permute-start.2 = (f32[2,96,128]{2,1,0:T(8,128)S(1)}, f32[2,96,128]{2,1,0:T(8,128)S(1)}, u32[]{:S(2)}, u32[]{:S(2)}) collective-permute-start(f32[2,96,128]{2,1,0:T(8,128)S(1)} %maximum_select_fusion.1), channel_id=1, source_target_pairs={{12,16},{16,12},{13,17},{17,13},{14,18},{18,14},{15,19},{19,15}} | collective-permute-start | bytes 294920 | tf_op jit(solution)/shard_map/ppermute | solution.py:419
  11.1 0.9 %copy-start.6 = (s32[1,1,1,4,512]{4,3,2,1,0:T(4,128)S(1)}, s32[1,1,1,4,512]{4,3,2,1,0:T(4,128)}, u32[]{:S(2)}) copy-start(s32[1,1,1,4,512]{4,3,2,1,0:T(4,128)} %param.11) | copy-start | bytes 24580
  11.1 1.6 %copy-start.3 = (f32[1,1,1,12,2560]{4,2,3,1,0:T(1,128)S(1)}, f32[1,1,1,12,2560]{4,2,3,1,0:T(1,128)}, u32[]{:S(2)}) copy-start(f32[1,1,1,12,2560]{4,2,3,1,0:T(1,128)} %param.16) | copy-start | bytes 368644
  11.1 0.8 %copy-start.8 = (s32[1,1,1,6,256]{4,2,3,1,0:T(1,128)S(1)}, s32[1,1,1,6,256]{4,2,3,1,0:T(1,128)}, u32[]{:S(2)}) copy-start(s32[1,1,1,6,256]{4,2,3,1,0:T(1,128)} %param.14) | copy-start | bytes 18436
  11.1 8.9 %collective-permute-start.1 = (f32[2,96,128]{2,1,0:T(8,128)S(1)}, f32[2,96,128]{2,1,0:T(8,128)S(1)}, u32[]{:S(2)}, u32[]{:S(2)}) collective-permute-start(f32[2,96,128]{2,1,0:T(8,128)S(1)} %maximum_select_fusion), channel_id=1, source_target_pairs={{8,16},{16,8},{12,20},{20,12},{9,17},{17,9},{13,21},{21,13},{10,18... | collective-permute-start | bytes 294920 | tf_op jit(solution)/shard_map/ppermute | solution.py:418
  12.0 0.7 %copy-start.7 = (f32[1,1,1,4,512]{4,3,2,1,0:T(4,128)S(1)}, f32[1,1,1,4,512]{4,3,2,1,0:T(4,128)}, u32[]{:S(2)}) copy-start(f32[1,1,1,4,512]{4,3,2,1,0:T(4,128)} %param.12) | copy-start | bytes 24580
  13.0 0.8 %copy-start.4 = (s32[1,1,1,4,2560]{4,3,2,1,0:T(4,128)S(1)}, s32[1,1,1,4,2560]{4,3,2,1,0:T(4,128)}, u32[]{:S(2)}) copy-start(s32[1,1,1,4,2560]{4,3,2,1,0:T(4,128)} %param.15) | copy-start | bytes 122884
  13.8 0.7 %copy-start.5 = (f32[1,1,1,2560]{3,2,1,0:T(1,128)S(1)}, f32[1,1,1,2560]{3,2,1,0:T(1,128)}, u32[]{:S(2)}) copy-start(f32[1,1,1,2560]{3,2,1,0:T(1,128)} %param.17) | copy-start | bytes 30724
  17.8 2.3 %copy-start.2 = (s32[1,1,1,512]{3,2,1,0:T(1,128)S(1)}, s32[1,1,1,512]{3,2,1,0:T(1,128)}, u32[]{:S(2)}) copy-start(s32[1,1,1,512]{3,2,1,0:T(1,128)} %param.13) | copy-start | bytes 6148
  21.4 16.0 %collective-permute-start.3 = (f32[12,128]{1,0:T(8,128)S(1)}, f32[12,128]{1,0:T(8,128)S(1)}, u32[]{:S(2)}, u32[]{:S(2)}) collective-permute-start(f32[12,128]{1,0:T(8,128)S(1)} %get-tuple-element.18), channel_id=1, source_target_pairs={{4,8},{8,4},{12,16},{16,12},{20,24},{24,20},{5,9},{9,5},{13,17},{1... | collective-permute-start | bytes 18440 | tf_op jit(solution)/shard_map/ppermute | solution.py:70
  41.2 12.1 %collective-permute-start.4 = (f32[8,128]{1,0:T(8,128)S(1)}, f32[8,128]{1,0:T(8,128)S(1)}, u32[]{:S(2)}, u32[]{:S(2)}) collective-permute-start(f32[8,128]{1,0:T(8,128)S(1)} %get-tuple-element.21), channel_id=1, source_target_pairs={{4,8},{8,4},{12,16},{16,12},{20,24},{24,20},{5,9},{9,5},{13,17},{1... | collective-permute-start | bytes 12296 | tf_op jit(solution)/shard_map/ppermute | solution.py:70
